TPU v7x, 512 devices: a whole 4x4x16 slice. The times are simulated.
512 devices in a mesh: grp: 16 (over z_hi, y, core), inp: 32 (over z_lo, x).
Axes of the slice: x: 4, y: 4, z: 16 (z_hi: 2, z_lo: 8; z = z_hi * 8 + z_lo), core: 2. Of those that a mesh axis runs over, the one named last changes fastest.
Arguments:
- samples: bfloat16 [512, 2097152], P('inp', 'grp'), may hold values from -6 to 6
- channel_index: int32 [128], replicated, may hold values from 0 to 1023, as said below
- tile_order: int32 [10, 2], replicated, may hold values from 0 to 3, as said below
Outputs:
- visibility: float32 [128, 10, 2, 128, 128], P('inp', None, None, 'grp')
Inputs may be any that keep to these rules, and one draw needn't show every extreme that they name: `channel_index`: 128 distinct channel numbers. `tile_order`: each pair (r, q) of tiles with r >= q, of the 4 tiles of streams, appears exactly once.
All inputs are finite; a program needn't handle non-finite values.
Results may differ from a plain program's by a relative error of at most 0.013.
Values may be sent and summed in bfloat16 or wider, within the bound.
A program may use at most 64 MiB of HBM per device.

v0:
```python
import math

import jax
import jax.numpy as jnp
from jax import lax
from jax.sharding import PartitionSpec as P

FFT = 2048
TAPS = 16
TILE = 128


def from_behind(value, axis, by):
    length = lax.axis_size(axis)
    pairs = [(i, i + by) for i in range(length) if 0 <= i + by < length]
    return lax.ppermute(value, axis, pairs)


def pfb_window():
    length = TAPS * FFT
    position = jnp.arange(length, dtype=jnp.int32).astype(jnp.float32)
    offset = (position - length // 2 + 0.5) / FFT
    sinc_part = jnp.sin(math.pi * offset) / (math.pi * offset)
    hamming = 0.54 - 0.46 * jnp.cos(2.0 * math.pi * position / (length - 1))
    shaped = (sinc_part * hamming).reshape(TAPS, FFT)
    power_mean = jnp.sum(shaped * shaped) / FFT
    return shaped / jnp.sqrt(power_mean)


def channel_table(channel_index, peer_count):
    column = jnp.arange(FFT, dtype=jnp.int32)
    phase_index = channel_index[:, None] * column[None, :] % FFT
    angles = 2.0 * math.pi / FFT * phase_index.astype(jnp.float32)
    scaling = 1.0 / math.sqrt(FFT)
    dft_rows = jnp.stack([jnp.cos(angles) * scaling, -jnp.sin(angles) * scaling], axis=1).astype(
        jnp.bfloat16
    )
    per_peer = dft_rows.shape[0] // peer_count
    return jnp.transpose(dft_rows.reshape(peer_count, per_peer, 2, FFT), (1, 0, 2, 3))


def products(voltages, tile_order):
    item_count = voltages.shape[0]
    streams_all = voltages.shape[1]
    full_width = voltages.shape[2]
    half_width = full_width // 2
    blocks_count = streams_all // TILE
    turned = jnp.concatenate([voltages[..., half_width:], -voltages[..., :half_width]], axis=-1)
    stacked = jnp.stack([voltages, turned], axis=1).reshape(
        item_count, 2, blocks_count, TILE, full_width
    )
    right_rows = voltages.reshape(item_count, blocks_count, TILE, full_width)
    square = jnp.einsum(
        "ckiaf,cjbf->ckiajb", stacked, right_rows, preferred_element_type=jnp.float32
    )
    picked = square[:, :, tile_order[:, 0], :, tile_order[:, 1], :]
    return jnp.transpose(picked, (1, 0, 2, 3, 4))


def shards(samples, channel_index, tile_order):
    peer_count = lax.axis_size("inp")
    group_count = lax.axis_size("grp")
    streams_here = samples.shape[0]
    frames_here = samples.shape[1] // FFT
    window = pfb_window()
    history = (TAPS - 1) * FFT
    earlier = from_behind(samples[:, samples.shape[1] - history :], "grp", 1)
    padded = jnp.concatenate([earlier, samples], axis=1).reshape(
        streams_here, frames_here + TAPS - 1, FFT
    )
    filtered = jnp.zeros((streams_here, frames_here, FFT), jnp.float32)
    for tap_index in range(TAPS):
        filtered = filtered + window[tap_index] * padded[
            :, tap_index : tap_index + frames_here
        ].astype(jnp.float32)
    filtered = filtered.astype(jnp.bfloat16)
    dft_rows = channel_table(channel_index, peer_count)
    channel_local = dft_rows.shape[0]
    spectra = jnp.einsum("rqkp,sfp->rqskf", dft_rows, filtered, preferred_element_type=jnp.float32)
    spectra = spectra.reshape(channel_local, peer_count, streams_here, 2 * frames_here).astype(
        jnp.bfloat16
    )
    scaling = 1.0 / math.sqrt(frames_here * group_count)
    partial_terms = (
        products(
            lax.all_to_all(spectra, "inp", split_axis=1, concat_axis=2, tiled=True)[:, 0],
            tile_order,
        )
        * scaling
    )
    return lax.psum_scatter(
        partial_terms.astype(jnp.bfloat16), "grp", scatter_dimension=3, tiled=True
    ).astype(jnp.float32)


def solution(mesh):
    in_specs = (P("inp", "grp"), P(), P())
    out_specs = P("inp", None, None, "grp", None)
    return jax.shard_map(shards, mesh=mesh, in_specs=in_specs, out_specs=out_specs, check_vma=False)
```

profile of v0, /device:TPU:1, one launch (start us, length us, event | category | flops | bytes accessed | tf_op | source)
XLA Modules:
  0.0 309.5 jit_solution(6810166843239853811)
XLA Ops:
  6.5 1.3 slice.112
  7.8 4.6 %collective-permute-start = (bf16[16,30720]{1,0:T(8,128)(2,1)S(1)}, bf16[16,30720]{1,0:T(8,128)(2,1)S(1)}, u32[]{:S(2)}, u32[]{:S(2)}) collective-permute-start(bf16[16,30720]{1,0:T(8,128)(2,1)S(1)} %slice.112), channel_id=1, source_target_pairs={{0,32},{32,64},{64,96},{96,128},{128,160},{160,192},{192,224},{224... | collective-permute-start | bytes 2949128 | tf_op jit(solution)/shard_map/ppermute | solution.py:16
  12.4 1.5 fusion.24
  14.6 0.9 fusion.21
  15.5 0.8 mul.334
  16.3 0.1 copy.15
  16.3 0.1 fusion.34
  16.4 4.9 %multiply_convert_fusion.2 = (bf16[32,4,1,2048]{3,0,2,1:T(8,128)(2,1)S(1)}, bf16[32,4,1,2048]{3,0,2,1:T(8,128)(2,1)S(1)}) fusion(s32[32,4]{0,1:T(4,128)S(1)} %copy.15), kind=kLoop, calls=%fused_computation.24 | loop fusion | flops 4980736 | bytes 1049088 | tf_op jit(solution)/shard_map/convert
  21.4 2.1 collective-permute-done
  23.4 6.7 %pad_maximum_fusion = bf16[16,161792]{1,0:T(8,128)(2,1)} fusion(bf16[16,131072]{1,0:T(8,128)(2,1)} %param.3, bf16[16,30720]{1,0:T(8,128)(2,1)S(1)} %collective-permute-done), kind=kLoop, calls=%fused_computation.3 | loop fusion | flops 10354688 | bytes 10354688 | tf_op jit(solution)/shard_map/concatenate | solution.py:68
  30.1 6.1 %reshape.128 = bf16[16,79,2048]{2,1,0:T(8,128)(2,1)} reshape(bf16[16,161792]{1,0:T(8,128)(2,1)} %pad_maximum_fusion) | data formatting | bytes 10354688 | tf_op jit(solution)/shard_map/reshape | solution.py:68
  36.2 0.0 copy-start
  36.2 41.6 %fusion.6 = bf16[4,32,16,2,64]{4,1,3,0,2:T(8,128)(2,1)S(1)} fusion(bf16[16,79,2048]{2,1,0:T(8,128)(2,1)} %reshape.128, f32[2048]{0:T(1024)S(1)} %bitcast.64, f32[2048]{0:T(1024)S(1)} %bitcast.65, f32[2048]{0:T(1024)S(1)} %bitcast.66, f32[2048]{0:T(1024)S(1)} %bitcast.67, f32[2048]{0:T(1024)S(1)} %bitcast.68, f32[2048]{0:T(1024)S(1)} %bitcast.69, ...), kind=kOutput, calls=%fused_computation.12 | convolution fusion | flops 1176764416 | bytes 68812800 | tf_op jit(solution)/shard_map/rqkp,sfp->rqskf/dot_general | solution.py:79
  77.9 1.1 copy.25
  79.0 1.3 reshape.139
  80.3 15.1 %all-to-all-start = ((bf16[4,32,16,128]{3,2,0,1:T(8,128)(2,1)}), bf16[4,32,16,128]{3,2,0,1:T(8,128)(2,1)S(1)}, u32[]{:S(2)}, u32[]{:S(2)}) async-start(bf16[4,32,16,128]{3,2,0,1:T(8,128)(2,1)} %reshape.139), calls=%async_computation | async-start | bytes 1048576 | tf_op jit(solution)/shard_map/all_to_all | solution.py:86
  95.4 0.3 reduce-scatter.4.cloned.1.call-start
  95.7 0.0 copy-done
  95.7 27.0 %all-to-all-done = bf16[4,32,16,128]{3,2,0,1:T(8,128)(2,1)S(1)} async-done(((bf16[4,32,16,128]{3,2,0,1:T(8,128)(2,1)}), bf16[4,32,16,128]{3,2,0,1:T(8,128)(2,1)S(1)}, u32[]{:S(2)}, u32[]{:S(2)}) %all-to-all-start) | async-done | bytes 524320 | tf_op jit(solution)/shard_map/all_to_all | solution.py:86
  122.7 0.2 fusion.33
  123.0 0.3 pad_maximum_fusion.1
  123.3 4.5 %fusion.14 = f32[4,2,4,128,4,128]{5,3,4,2,1,0:T(8,128)} fusion(bf16[4,4,128,128,1,1]{3,2,1,5,4,0:T(8,128)(2,1)S(1)} %bitcast.58, bf16[4,1,4,128,128]{4,3,2,1,0:T(8,128)(2,1)S(1)} %bitcast.61, bf16[4,1,4,128,128]{4,3,2,1,0:T(8,128)(2,1)S(1)} %bitcast.59), kind=kOutput, calls=%fused_computation.20 | convolution fusion | flops 538968064 | bytes 9961472 | tf_op jit(solution)/shard_map/ckiaf,cjbf->ckiajb/dot_general | solution.py:53
  127.7 6.8 %gather_fusion = f32[10,4,2,128,128]{4,3,2,1,0:T(8,128)} fusion(f32[4,2,4,128,4,128]{5,3,4,2,1,0:T(8,128)} %fusion.14, s32[10]{0:T(128)S(1)} %fusion.30), kind=kCustom, calls=%fused_computation | custom fusion | bytes 10485840 | tf_op jit(solution)/shard_map/gather | solution.py:56
  134.6 3.2 %fusion.2 = bf16[4,10,2,128,128]{4,3,2,0,1:T(8,128)(2,1)S(1)} fusion(f32[10,4,2,128,128]{4,3,2,1,0:T(8,128)} %gather_fusion), kind=kLoop, calls=%fused_computation.6 | loop fusion | flops 2621440 | bytes 7864320 | tf_op jit(solution)/shard_map/convert_element_type | solution.py:92
  137.8 2.7 copy.31
  140.5 3.2 %reshape.140 = bf16[128,10240]{1,0:T(8,128)(2,1)} reshape(bf16[128,10,4,2,128]{4,3,2,1,0:T(2,128)(2,1)S(1)} %bitcast.60) | data formatting | bytes 5242880
  143.6 0.0 reduce-scatter.4.cloned.1.call-update
  143.6 157.2 %reduce-scatter.4.cloned.1.call-done = bf16[8,10240]{1,0:T(8,128)(2,1)} async-done(((bf16[128,10240]{1,0:T(8,128)(2,1)}), bf16[8,10240]{1,0:T(8,128)(2,1)}) %reduce-scatter.4.cloned.1.call-update) | async-done | bytes 163856
  300.9 1.0 reshape.141
  301.9 0.7 copy.21
  (3 shorter events, 0.1 us)
Async XLA Ops:
  7.8 15.6 %collective-permute-start = (bf16[16,30720]{1,0:T(8,128)(2,1)S(1)}, bf16[16,30720]{1,0:T(8,128)(2,1)S(1)}, u32[]{:S(2)}, u32[]{:S(2)}) collective-permute-start(bf16[16,30720]{1,0:T(8,128)(2,1)S(1)} %slice.112), channel_id=1, source_target_pairs={{0,32},{32,64},{64,96},{96,128},{128,160},{160,192},{192,224},{224... | collective-permute-start | bytes 2949128 | tf_op jit(solution)/shard_map/ppermute | solution.py:16
  36.2 59.4 %copy-start = (s32[10,2]{0,1:T(2,128)S(1)}, s32[10,2]{0,1:T(2,128)}, u32[]{:S(2)}) copy-start(s32[10,2]{0,1:T(2,128)} %param.5) | copy-start | bytes 244
  80.3 42.4 %all-to-all-start = ((bf16[4,32,16,128]{3,2,0,1:T(8,128)(2,1)}), bf16[4,32,16,128]{3,2,0,1:T(8,128)(2,1)S(1)}, u32[]{:S(2)}, u32[]{:S(2)}) async-start(bf16[4,32,16,128]{3,2,0,1:T(8,128)(2,1)} %reshape.139), calls=%async_computation | async-start | bytes 1048576 | tf_op jit(solution)/shard_map/all_to_all | solution.py:86
  95.4 205.5 %reduce-scatter.4.cloned.1.call-start = ((), (), s32[]{:S(2)}) async-start(), calls=%async_computation.2 | async-start | bytes 2785280
Sparse Core Ops, SparseCore 0:
  143.8 157.0 reduce-scatter.3
where the time goes:
time: 311 us; the launch traced here: 310 us
  waiting for transfers between devices  186 us (60%)
  matrix products  46.1 us (15%)
  local copies, waits for them, and re-layouts  25.2 us (8%)
  starting transfers between devices  20 us (6%)
  other arithmetic  17.7 us (6%)
  between operations  14.2 us (5%)
    unnamed x2, waiting for transfers between devices  157 us
    dot_general x1, matrix products, shards(): jnp.einsum('rqkp,sfp->rqskf', dft_rows, filtered, preferred_element_type=...  41.6 us
    all_to_all x1, waiting for transfers between devices, shards(): lax.all_to_all(spectra, 'inp', split_axis=1, concat_axis=2, tiled=True)  27 us
    all_to_all x1, starting transfers between devices, shards(): lax.all_to_all(spectra, 'inp', split_axis=1, concat_axis=2, tiled=True)  15.1 us
    unnamed x5, local copies, waits for them, and re-layouts  6.86 us
    gather x1, local copies, waits for them, and re-layouts, products(): picked = square[:, :, tile_order[:, 0], :, tile_order[:, 1], :]  6.85 us
    concatenate x1, other arithmetic, shards(): jnp.concatenate([earlier, samples], axis=1)  6.66 us
  transfers between devices with their start and end apart: 3, of which 3 were waited for; matrix products, arithmetic and copies ran while one was open for 3% of the time, Pallas kernels for 0%

commit v1 on v0

v1 whole, which is shorter than its diff:
```python
import math

import jax
import jax.numpy as jnp
import numpy as np
from jax import lax
from jax.experimental import pallas as pl
from jax.experimental.pallas import tpu as pltpu
from jax.sharding import PartitionSpec as P

FFT = 2048
TAPS = 16
TILE = 128
LANES = 128
MESH = pl.DeviceIdType.MESH
F32 = jnp.float32
BF16 = jnp.bfloat16
VMEM = pl.BlockSpec(memory_space=pltpu.VMEM)
LIMIT = 48 * 1024 * 1024


def pfb_window():
    length = TAPS * FFT
    position = np.arange(length, dtype=np.float64)
    offset = (position - length // 2 + 0.5) / FFT
    shaped = np.sinc(offset) * (0.54 - 0.46 * np.cos(2.0 * np.pi * position / (length - 1)))
    shaped = shaped / np.sqrt(np.sum(shaped * shaped) / FFT)
    return shaped.reshape(TAPS, FFT).astype(np.float32)


def nt_dot(a, b):
    return lax.dot_general(a, b, (((1,), (1,)), ((), ())), preferred_element_type=F32)


def wide(held, rows):
    return jnp.concatenate([held[a, rows].astype(BF16) for a in range(held.shape[0])], axis=1)


def fir(x_ref, taps, lane, first, count, frames):
    sums = [None] * count
    for frame in range(max(first - TAPS + 1, 0), min(first + count, frames)):
        value = x_ref[:, pl.ds(frame * FFT + lane, LANES)].astype(F32)
        for at in range(count):
            tap = frame - (first + at) + TAPS - 1
            if 0 <= tap < TAPS:
                term = taps[tap] * value
                sums[at] = term if sums[at] is None else sums[at] + term
    return sums


def load_taps(w_ref, lane):
    return [w_ref[pl.ds(k, 1), pl.ds(lane, LANES)] for k in range(TAPS)]


def table_and_tail_kernel(index_ref, x_ref, w_ref, table_ref, tail_ref, held):
    channels = index_ref.shape[1]
    streams = x_ref.shape[0]
    frames = x_ref.shape[1] // FFT
    step = 2.0 * math.pi / FFT
    channel = jnp.transpose(jnp.broadcast_to(index_ref[...], (channels, channels)))
    column = lax.broadcasted_iota(jnp.int32, (channels, channels), 1)
    fine = ((channel * column) % FFT).astype(F32) * step
    coarse = ((channel * (column * LANES)) % FFT).astype(F32) * step
    scale = 1.0 / math.sqrt(FFT)
    fine_cos, fine_sin = jnp.cos(fine) * scale, jnp.sin(fine) * scale
    coarse_cos, coarse_sin = jnp.cos(coarse), jnp.sin(coarse)
    for a in range(FFT // LANES):
        c, s = coarse_cos[:, a : a + 1], coarse_sin[:, a : a + 1]
        lanes = slice(a * LANES, (a + 1) * LANES)
        table_ref[0:channels, lanes] = (c * fine_cos - s * fine_sin).astype(BF16)
        table_ref[channels:, lanes] = (-(s * fine_cos + c * fine_sin)).astype(BF16)

    def chunk(at, carry):
        lane = pl.multiple_of(at * LANES, LANES)
        taps = load_taps(w_ref, lane)
        for first in (0, 8):
            sums = fir(x_ref, taps, lane, frames + first, 8, frames)
            for o, value in enumerate(sums):
                if value is None:
                    value = jnp.zeros((streams, LANES), F32)
                held[at, pl.ds(first + o, streams, stride=TAPS), :] = value
        return carry

    lax.fori_loop(0, FFT // LANES, chunk, 0)
    tail_ref[...] = nt_dot(table_ref[...], wide(held, slice(None))).astype(BF16)


def main_kernel(table_ref, x_ref, w_ref, out_ref, held):
    streams = x_ref.shape[0]
    frames = x_ref.shape[1] // FFT

    def chunk(at, carry):
        lane = pl.multiple_of(at * LANES, LANES)
        taps = load_taps(w_ref, lane)
        for first in range(0, frames, 8):
            sums = fir(x_ref, taps, lane, first, 8, frames)
            for o, value in enumerate(sums):
                held[at, pl.ds(first + o, streams, stride=frames), :] = value
        return carry

    lax.fori_loop(0, FFT // LANES, chunk, 0)
    for part in range(out_ref.shape[0]):
        rows = slice(part * 4 * frames, (part + 1) * 4 * frames)
        out_ref[part] = nt_dot(table_ref[...], wide(held, rows))


def exchange_kernel(
    d_ref, t_ref, out_ref, stage, send, v, p, r1, r2, keep, s3, r3, a_send, a_recv, c_send, c_recv, y_send, y_recv, z_send, z_recv
):
    channels, peers = v.shape[0], lax.axis_size("inp")
    me, g = lax.axis_index("inp"), lax.axis_index("grp")
    core, y, z = g % 2, (g // 2) % 4, g // 8
    rows = out_ref.shape[1]
    frames = LANES // 2

    barrier = pltpu.get_barrier_semaphore()

    def greet(d, carry):
        pl.semaphore_signal(barrier, inc=1, device_id={"inp": lax.rem(me + d, peers)}, device_id_type=MESH)
        return carry

    def y_peer(d):
        return z * 8 + ((y + d) % 4) * 2 + core

    core_peer = g + 1 - 2 * core
    z_peer = (1 - z) * 8 + y * 2 + core
    lax.fori_loop(1, peers, greet, 0)
    for other in (core_peer, y_peer(1), y_peer(2), y_peer(3), z_peer):
        pl.semaphore_signal(barrier, inc=1, device_id={"grp": other}, device_id_type=MESH)

    total = d_ref.shape[1] // 2
    source = lax.broadcasted_iota(jnp.int32, (256, 256), 0)
    target = lax.broadcasted_iota(jnp.int32, (256, 256), 1)
    low = lax.broadcasted_iota(jnp.int32, (total, LANES), 1) < frames
    for part in range(d_ref.shape[0]):
        same = (source // TAPS == target // frames + part * 4) & (source % TAPS == target % frames)
        spectra = d_ref[part] + jnp.dot(t_ref[...], same.astype(F32).astype(BF16), preferred_element_type=F32)
        for pair in range(2):
            re = spectra[0:total, pair * LANES : (pair + 1) * LANES]
            im = spectra[total:, pair * LANES : (pair + 1) * LANES]
            stream = part * 4 + pair * 2
            stage[pl.ds(stream, total, stride=16), :] = jnp.where(low, re, pltpu.roll(im, frames, 1))
            stage[pl.ds(stream + 1, total, stride=16), :] = jnp.where(low, pltpu.roll(re, frames, 1), im)
    send[...] = stage[...].astype(BF16)

    pl.semaphore_wait(barrier, peers - 1 + 5)

    def turn(c):
        def one(d, carry):
            j = lax.rem(me + d, peers)
            pltpu.make_async_remote_copy(
                src_ref=send.at[pl.ds(pl.multiple_of((j * channels + c) * 16, 16), 16)],
                dst_ref=v.at[c, pl.ds(pl.multiple_of(me * 16, 16), 16)],
                send_sem=a_send.at[c],
                recv_sem=a_recv.at[c],
                device_id={"inp": j},
                device_id_type=MESH,
            ).start()
            return carry

        lax.fori_loop(1, peers, one, 0)

    def turn_wait(c, sem):
        part = v.at[c, pl.ds(0, (peers - 1) * 16)]
        pltpu.make_async_copy(part, part, sem.at[c]).wait()

    def core_copy(c):
        return pltpu.make_async_remote_copy(
            src_ref=p.at[c, 1 - core],
            dst_ref=r1.at[c],
            send_sem=c_send.at[c],
            recv_sem=c_recv.at[c],
            device_id={"grp": core_peer},
            device_id_type=MESH,
        )

    def y_copy(c, d):
        return pltpu.make_async_remote_copy(
            src_ref=p.at[c, core, (y + d) % 4],
            dst_ref=r2.at[c, d - 1],
            send_sem=y_send.at[c, d - 1],
            recv_sem=y_recv.at[c, d - 1],
            device_id={"grp": y_peer(d)},
            device_id_type=MESH,
        )

    def z_copy(c):
        return pltpu.make_async_remote_copy(
            src_ref=s3.at[c],
            dst_ref=r3.at[c],
            send_sem=z_send.at[c],
            recv_sem=z_recv.at[c],
            device_id={"grp": z_peer},
            device_id_type=MESH,
        )

    for c in range(channels):
        turn(c)
    sign = jnp.where(lax.broadcasted_iota(jnp.int32, (TILE, LANES), 1) < frames, 1.0, -1.0) / 32.0
    tiles = v.shape[1] // TILE

    def products(c):
        for r in range(tiles):
            value = v[c, r * TILE : (r + 1) * TILE].astype(F32)
            turned = (pltpu.roll(value, frames, 1) * sign).reshape(16, 8, LANES)
            value = (value / 32.0).reshape(16, 8, LANES)
            order = [zz * 8 + yy * 2 + cc for cc in range(2) for yy in range(4) for zz in range(2)]
            left = jnp.concatenate([part for o in order for part in (value[o], turned[o])], axis=0).astype(BF16)
            for q in range(r + 1):
                t = r * (r + 1) // 2 + q
                got = nt_dot(left, v[c, q * TILE : (q + 1) * TILE]).astype(BF16)
                p[c, :, :, :, t * 16 : (t + 1) * 16, :] = got.reshape(2, 4, 2, 16, LANES)

    def core_sum(c):
        core_copy(c).wait_recv()
        for yy in range(4):
            p[c, core, yy] = (p[c, core, yy].astype(F32) + r1[c, yy].astype(F32)).astype(BF16)
        for d in range(1, 4):
            y_copy(c, d).start()

    def y_sum(c):
        for d in range(1, 4):
            y_copy(c, d).wait_recv()
        for zz in (z, 1 - z):
            got = p[c, core, y, zz].astype(F32)
            for d in range(3):
                got = got + r2[c, d, zz].astype(F32)
            if zz is z:
                keep[c] = got
            else:
                s3[c] = got.astype(BF16)
        z_copy(c).start()

    for c in range(channels):
        turn_wait(c, a_recv)
        own = pl.multiple_of((me * channels + c) * 16, 16)
        v[c, pl.ds(pl.multiple_of(me * 16, 16), 16)] = send[pl.ds(own, 16)]
        products(c)
        core_copy(c).start()
        if c:
            y_sum(c - 1)
        core_sum(c)
    y_sum(channels - 1)
    for c in range(channels):
        z_copy(c).wait_recv()
        out_ref[c] = keep[c] + r3[c].astype(F32)
    for c in range(channels):
        turn_wait(c, a_send)
        core_copy(c).wait_send()
        for d in range(1, 4):
            y_copy(c, d).wait_send()
        z_copy(c).wait_send()


def order_kernel(order_ref, in_ref, out_ref):
    for t in range(out_ref.shape[1]):
        r, q = order_ref[2 * t], order_ref[2 * t + 1]
        at = r * (r + 1) // 2 + q
        out_ref[:, pl.ds(t, 1)] = in_ref[:, pl.ds(at, 1)]


def table_and_tail(samples, channel_index, window):
    streams, selected = samples.shape[0], channel_index.shape[0]
    return pl.pallas_call(
        table_and_tail_kernel,
        out_shape=(
            jax.ShapeDtypeStruct((2 * selected, FFT), BF16),
            jax.ShapeDtypeStruct((2 * selected, streams * TAPS), BF16),
        ),
        in_specs=[VMEM] * 3,
        out_specs=(VMEM, VMEM),
        scratch_shapes=[pltpu.VMEM((FFT // LANES, streams * TAPS, LANES), F32)],
        compiler_params=pltpu.CompilerParams(vmem_limit_bytes=LIMIT),
        name="table_and_tail",
    )(channel_index.reshape(1, selected), samples, window)


def filter_and_dft(table, samples, window):
    streams, selected, frames = samples.shape[0], table.shape[0] // 2, samples.shape[1] // FFT
    return pl.pallas_call(
        main_kernel,
        out_shape=jax.ShapeDtypeStruct((streams // 4, 2 * selected, 4 * frames), F32),
        in_specs=[VMEM] * 3,
        out_specs=VMEM,
        scratch_shapes=[pltpu.VMEM((FFT // LANES, streams * frames, LANES), F32)],
        compiler_params=pltpu.CompilerParams(vmem_limit_bytes=LIMIT),
        cost_estimate=pl.CostEstimate(flops=2 * streams * frames * FFT * (TAPS + 2 * selected), bytes_accessed=8 << 20, transcendentals=0),
        name="filter_and_dft",
    )(table, samples, window)


def shards(samples, channel_index, tile_order):
    streams, length = samples.shape
    selected = channel_index.shape[0]
    peers = lax.axis_size("inp")
    group = lax.axis_size("grp")
    channels = selected // peers
    tile_count = tile_order.shape[0]
    window = jnp.asarray(pfb_window())

    table, tail = table_and_tail(samples, channel_index, window)
    earlier = lax.ppermute(tail, "grp", [(i, i + 1) for i in range(group - 1)])
    main = filter_and_dft(table, samples, window)
    dma = pltpu.SemaphoreType.DMA
    rows = tile_count * 16
    summed = pl.pallas_call(
        exchange_kernel,
        out_shape=jax.ShapeDtypeStruct((channels, rows, LANES), F32),
        in_specs=[VMEM] * 2,
        out_specs=VMEM,
        scratch_shapes=[
            pltpu.VMEM((selected * streams, LANES), F32),
            pltpu.VMEM((selected * streams, LANES), BF16),
            pltpu.VMEM((channels, peers * streams, LANES), BF16),
            pltpu.VMEM((channels, 2, 4, 2, rows, LANES), BF16),
            pltpu.VMEM((channels, 4, 2, rows, LANES), BF16),
            pltpu.VMEM((channels, 3, 2, rows, LANES), BF16),
            pltpu.VMEM((channels, rows, LANES), F32),
            pltpu.VMEM((channels, rows, LANES), BF16),
            pltpu.VMEM((channels, rows, LANES), BF16),
            dma((channels,)),
            dma((channels,)),
            dma((channels,)),
            dma((channels,)),
            dma((channels, 3)),
            dma((channels, 3)),
            dma((channels,)),
            dma((channels,)),
        ],
        compiler_params=pltpu.CompilerParams(collective_id=0, has_side_effects=True, vmem_limit_bytes=LIMIT),
        name="exchange",
    )(main, earlier)
    return pl.pallas_call(
        order_kernel,
        out_shape=jax.ShapeDtypeStruct((channels, tile_count, 2, 8, LANES), F32),
        in_specs=[pl.BlockSpec(memory_space=pltpu.SMEM), VMEM],
        out_specs=VMEM,
        name="tile_order",
    )(tile_order.reshape(-1), summed.reshape(channels, tile_count, 2, 8, LANES))


def solution(mesh):
    in_specs = (P("inp", "grp"), P(), P())
    out_specs = P("inp", None, None, "grp", None)
    return jax.shard_map(shards, mesh=mesh, in_specs=in_specs, out_specs=out_specs, check_vma=False)
```

time: 311 us -> 91.8 us (0.30)
  the two profiles are of different devices: /device:TPU:1 before, /device:TPU:52 now
where the time goes in v1:
time: 91.8 us; the launch traced here: 91.5 us
  Pallas kernels  84.3 us (92%)
  local copies, waits for them, and re-layouts  5.24 us (6%)
  starting transfers between devices  1.92 us (2%)
    pallas_call x1, Pallas kernels, shards(): pl.pallas_call(exchange_kernel, out_shape=jax.ShapeDtypeStruct((channels,...  65.2 us
    pallas_call x1, Pallas kernels, filter_and_dft(): pl.pallas_call(main_kernel, out_shape=jax.ShapeDtypeStruct((streams // 4,...  14.3 us
    unnamed x13, local copies, waits for them, and re-layouts  4.58 us
    pallas_call x1, Pallas kernels, table_and_tail(): pl.pallas_call(table_and_tail_kernel, out_shape=(jax.ShapeDtypeStruct((2...  3.03 us
    ppermute x1, starting transfers between devices, shards(): earlier = lax.ppermute(tail, 'grp', [(i, i + 1) for i in range(group - 1)])  1.92 us
  transfers between devices with their start and end apart: 1, of which 0 were waited for; matrix products, arithmetic and copies ran while one was open for 1% of the time, Pallas kernels for 16%

profile of v1, /device:TPU:52, one launch (start us, length us, event | category | flops | bytes accessed | tf_op | source)
XLA Modules:
  0.0 91.5 jit_solution(15938878278904549755)
XLA Ops:
  0.0 0.0 copy-start.5
  0.0 0.0 copy-start
  0.0 2.2 %copy-done = bf16[16,131072]{1,0:T(8,128)(2,1)S(1)} copy-done((bf16[16,131072]{1,0:T(8,128)(2,1)S(1)}, bf16[16,131072]{1,0:T(8,128)(2,1)}, u32[]{:S(2)}) %copy-start) | copy-done | bytes 4194328
  2.2 0.0 copy-start.2
  2.2 0.9 copy-done.2
  3.1 0.0 copy-start.4
  3.1 0.7 copy-done.4
  3.8 0.0 copy-start.3
  3.8 3.0 %table_and_tail.1 = (bf16[256,2048]{1,0:T(8,128)(2,1)S(1)}, bf16[256,256]{1,0:T(8,128)(2,1)S(1)}) custom-call(s32[1,128]{1,0:T(1,128)S(1)} %bitcast.3, bf16[16,131072]{1,0:T(8,128)(2,1)S(1)} %copy-done, f32[16,2048]{1,0:T(8,128)S(1)} %copy-done.2), custom_call_target="tpu_custom_call" | custom-call | tf_op jit(solution)/shard_map/table_and_tail/pallas_call | solution.py:264
  6.8 1.9 %collective-permute-start = (bf16[256,256]{1,0:T(8,128)(2,1)S(1)}, bf16[256,256]{1,0:T(8,128)(2,1)S(1)}, u32[]{:S(2)}, u32[]{:S(2)}) collective-permute-start(bf16[256,256]{1,0:T(8,128)(2,1)S(1)} %get-tuple-element.8), channel_id=1, source_target_pairs={{0,32},{32,64},{64,96},{96,128},{128,160},{160,192},{192,224},{224... | collective-permute-start | bytes 393224 | tf_op jit(solution)/shard_map/ppermute | solution.py:302
  8.7 0.0 copy-done.5
  8.7 0.1 copy.6
  8.8 0.7 reshape.9.order_ref
  9.5 0.0 copy-done.3
  9.5 14.3 %filter_and_dft.1.d_ref = f32[4,256,256]{2,1,0:T(8,128)S(1)} custom-call(bf16[256,2048]{1,0:T(8,128)(2,1)S(1)} %get-tuple-element.7.table_ref, bf16[16,131072]{1,0:T(8,128)(2,1)} %x_ref.3, f32[16,2048]{1,0:T(8,128)S(1)} %copy-done.3), custom_call_target="tpu_custom_call" | custom-call | flops 1140850688 | bytes 8388608 | tf_op jit(solution)/shard_map/filter_and_dft/pallas_call | solution.py:280
  23.8 0.0 collective-permute-done.t_ref
  23.8 65.2 %exchange.1 = f32[4,160,128]{2,1,0:T(8,128)S(1)} custom-call(f32[4,256,256]{2,1,0:T(8,128)S(1)} %filter_and_dft.1.d_ref, bf16[256,256]{1,0:T(8,128)(2,1)S(1)} %collective-permute-done.t_ref), custom_call_target="tpu_custom_call" | custom-call | tf_op jit(solution)/shard_map/exchange/pallas_call | solution.py:306
  89.0 0.0 copy-start.1
  89.0 0.7 copy-done.1
  89.8 1.8 %tile_order.1 = f32[4,10,2,8,128]{4,3,2,1,0:T(8,128)} custom-call(s32[20]{0:T(128)} %reshape.9.order_ref, f32[4,10,2,8,128]{4,3,2,1,0:T(8,128)} %bitcast.2), custom_call_target="tpu_custom_call" | custom-call | tf_op jit(solution)/shard_map/tile_order/pallas_call | solution.py:333
Async XLA Ops:
  0.0 8.7 %copy-start.5 = (s32[10,2]{0,1:T(2,128)S(1)}, s32[10,2]{0,1:T(2,128)}, u32[]{:S(2)}) copy-start(s32[10,2]{0,1:T(2,128)} %param.6) | copy-start | bytes 244
  0.0 2.2 %copy-start = (bf16[16,131072]{1,0:T(8,128)(2,1)S(1)}, bf16[16,131072]{1,0:T(8,128)(2,1)}, u32[]{:S(2)}) copy-start(bf16[16,131072]{1,0:T(8,128)(2,1)} %x_ref.3) | copy-start | bytes 12582916
  2.2 0.9 copy-start.2
  3.1 0.7 copy-start.4
  3.8 5.7 %copy-start.3 = (f32[16,2048]{1,0:T(8,128)S(1)}, f32[16,2048]{1,0:T(8,128)}, u32[]{:S(2)}) copy-start(f32[16,2048]{1,0:T(8,128)} %constant.2.clone.w_ref) | copy-start | bytes 393220
  6.8 17.0 %collective-permute-start = (bf16[256,256]{1,0:T(8,128)(2,1)S(1)}, bf16[256,256]{1,0:T(8,128)(2,1)S(1)}, u32[]{:S(2)}, u32[]{:S(2)}) collective-permute-start(bf16[256,256]{1,0:T(8,128)(2,1)S(1)} %get-tuple-element.8), channel_id=1, source_target_pairs={{0,32},{32,64},{64,96},{96,128},{128,160},{160,192},{192,224},{224... | collective-permute-start | bytes 393224 | tf_op jit(solution)/shard_map/ppermute | solution.py:302
  89.0 0.7 copy-start.1

commit v2 on v1

v2 whole, which is shorter than its diff:
```python
import math

import jax
import jax.numpy as jnp
import numpy as np
from jax import lax
from jax.experimental import pallas as pl
from jax.experimental.pallas import tpu as pltpu
from jax.sharding import PartitionSpec as P

FFT = 2048
TAPS = 16
TILE = 128
LANES = 128
CHUNKS = FFT // LANES
MESH = pl.DeviceIdType.MESH
F32 = jnp.float32
BF16 = jnp.bfloat16


def pfb_window():
    length = TAPS * FFT
    position = np.arange(length, dtype=np.float64)
    offset = (position - length // 2 + 0.5) / FFT
    shaped = np.sinc(offset) * (0.54 - 0.46 * np.cos(2.0 * np.pi * position / (length - 1)))
    shaped = shaped / np.sqrt(np.sum(shaped * shaped) / FFT)
    return shaped.reshape(TAPS, FFT).astype(np.float32)


def nt_dot(a, b):
    return lax.dot_general(a, b, (((1,), (1,)), ((), ())), preferred_element_type=F32)


def is_inner(tap):
    return TAPS // 2 - 2 <= tap < TAPS // 2 + 2


def fir(x_ref, w_ref, filt, at, first, count, row):
    streams, frames = x_ref.shape[0], x_ref.shape[1] // FFT
    lane = pl.multiple_of(at * LANES, LANES)
    taps = []
    for k in range(TAPS):
        weight = w_ref[pl.ds(k, 1), pl.ds(lane, LANES)]
        taps.append(weight if is_inner(k) else jnp.broadcast_to(weight, (streams, LANES)).astype(BF16))
    for start in range(first, first + count, 8):
        inner, outer = [None] * 8, [None] * 8
        for frame in range(max(start - TAPS + 1, 0), min(start + 8, frames)):
            value = x_ref[:, pl.ds(frame * FFT + lane, LANES)]
            wide = value.astype(F32)
            for o in range(8):
                tap = frame - (start + o) + TAPS - 1
                if not 0 <= tap < TAPS:
                    continue
                sums, term = (inner, taps[tap] * wide) if is_inner(tap) else (outer, taps[tap] * value)
                sums[o] = term if sums[o] is None else sums[o] + term
        for o in range(8):
            total = inner[o]
            if outer[o] is not None:
                total = outer[o].astype(F32) if total is None else total + outer[o].astype(F32)
            total = jnp.zeros((streams, LANES), F32) if total is None else total
            to = row + (start - first + o) * streams
            filt[to : to + streams, pl.ds(lane, LANES)] = total.astype(BF16)


def make_table(index_ref, picked, table):
    count = index_ref.shape[1]
    step = 2.0 * math.pi / FFT
    picked[...] = jnp.transpose(jnp.broadcast_to(index_ref[...], (count, count)))
    channel = jnp.concatenate([picked[pl.ds(i, count // 2, stride=2), :] for i in range(2)], axis=0)
    column = lax.broadcasted_iota(jnp.int32, (count, count), 1)
    fine = ((channel * column) & (FFT - 1)).astype(F32) * step
    coarse = ((channel * (column * LANES)) & (FFT - 1)).astype(F32) * step
    scale = 1.0 / math.sqrt(FFT)
    fine_cos, fine_sin = jnp.cos(fine) * scale, jnp.sin(fine) * scale
    coarse_cos, coarse_sin = jnp.cos(coarse), jnp.sin(coarse)
    for a in range(CHUNKS):
        c, s = coarse_cos[:, a : a + 1], coarse_sin[:, a : a + 1]
        lanes = slice(a * LANES, (a + 1) * LANES)
        table[0:count, lanes] = (c * fine_cos - s * fine_sin).astype(BF16)
        table[count : 2 * count, lanes] = (-(s * fine_cos + c * fine_sin)).astype(BF16)


def correlator_kernel(
    index_ref, order_ref, x_hbm, w_hbm, out_ref,
    x, w, picked, table, filt, dft, stage, send, tail, early, v, p, r1, r2, keep, s3, r3, done,
    load, t_sem, a_send, a_recv, c_send, c_recv, y_send, y_recv, z_send, z_recv,
):
    peers, groups = lax.axis_size("inp"), lax.axis_size("grp")
    channels = p.shape[0]
    me, g = lax.axis_index("inp"), lax.axis_index("grp")
    core, y, z = g % 2, (g // 2) % 4, g // 8
    streams, frames = x.shape[0], x.shape[1] // FFT
    half = frames // 2
    later = (g + 1) % groups

    def y_peer(d):
        return z * 8 + ((y + d) % 4) * 2 + core

    core_peer = g + 1 - 2 * core
    z_peer = (1 - z) * 8 + y * 2 + core
    across = (g + groups - 1 + 2 * core) % groups

    def fetch(number, first, count):
        part = pl.ds(first * FFT, count * FFT)
        return pltpu.make_async_copy(x_hbm.at[:, part], x.at[:, part], load.at[number])

    parts = [
        pltpu.make_async_copy(w_hbm, w, load.at[3]),
        fetch(0, frames - TAPS + 1, TAPS - 1),
        fetch(1, half - TAPS + 1, half),
        fetch(2, 0, half - TAPS + 1),
    ]
    for part in parts:
        part.start()

    barrier = pltpu.get_barrier_semaphore()

    def greet(d, carry):
        pl.semaphore_signal(barrier, inc=1, device_id={"inp": lax.rem(me + d, peers)}, device_id_type=MESH)
        return carry

    lax.fori_loop(1, peers, greet, 0)
    for other in (core_peer, y_peer(1), y_peer(2), y_peer(3), z_peer, across):
        pl.semaphore_signal(barrier, inc=1, device_id={"grp": other}, device_id_type=MESH)

    make_table(index_ref, picked, table)
    parts[0].wait()
    parts[1].wait()

    def filtered(first, count, lo=0, hi=CHUNKS):
        def chunk(at, carry):
            fir(x, w, filt, at, first, count, 0)
            return carry

        lax.fori_loop(lo, hi, chunk, 0)

    filtered(frames, TAPS)
    tail[...] = nt_dot(filt[0 : TAPS * streams, :], table[...]).astype(BF16)
    tail_copy = pltpu.make_async_remote_copy(
        src_ref=tail,
        dst_ref=early,
        send_sem=t_sem.at[0],
        recv_sem=t_sem.at[1],
        device_id={"grp": later},
        device_id_type=MESH,
    )
    parts[2].wait()
    filtered(half, half, 0, CHUNKS // 2)
    pl.semaphore_wait(barrier, peers - 1 + 6)

    @pl.when(g < groups - 1)
    def _():
        tail_copy.start()

    low = lax.broadcasted_iota(jnp.int32, (LANES // 2, LANES), 1) < LANES // 2

    def spectra(h):
        got = nt_dot(filt[...], table[...])
        if h == 0:
            got = jnp.concatenate([got[: TAPS * streams] + early[...].astype(F32), got[TAPS * streams :]], axis=0)
        dft[0] = got[:, :LANES]
        dft[1] = got[:, LANES:]
        for s in range(0, streams, 2):
            rows = [dft[k, pl.ds(s + i, half, stride=streams), :] for i in range(2) for k in range(2)]
            turned = jnp.transpose(jnp.concatenate(rows, axis=0))
            even, odd = turned[: LANES // 2], turned[LANES // 2 :]
            stage[pl.ds(s, LANES // 2, stride=streams), :] = jnp.where(low, even, pltpu.roll(odd, LANES // 2, 1))
            stage[pl.ds(s + 1, LANES // 2, stride=streams), :] = jnp.where(low, pltpu.roll(even, LANES // 2, 1), odd)
        send[h] = stage[...].astype(BF16)

    def turn(h, pair):
        def rows_of(j):
            return pl.ds(pl.multiple_of((j * 2 + pair) * streams, streams), streams)

        here = pl.ds(pl.multiple_of(me * streams, streams), streams)

        def one(d, carry):
            j = lax.rem(me + d, peers)
            pltpu.make_async_remote_copy(
                src_ref=send.at[h, rows_of(j)],
                dst_ref=v.at[h, pair, here],
                send_sem=a_send.at[h, pair],
                recv_sem=a_recv.at[h, pair],
                device_id={"inp": j},
                device_id_type=MESH,
            ).start()
            return carry

        lax.fori_loop(1, peers, one, 0)
        v[h, pair, here] = send[h, rows_of(me)]

    def turn_wait(h, pair, sem):
        part = v.at[h, pair, pl.ds(0, (peers - 1) * streams)]
        pltpu.make_async_copy(part, part, sem.at[h, pair]).wait()

    filtered(half, half, CHUNKS // 2, CHUNKS)
    spectra(1)
    turn(1, 0)
    turn(1, 1)
    parts[3].wait()
    filtered(0, half)

    @pl.when(g > 0)
    def _():
        tail_copy.wait_recv()

    @pl.when(g == 0)
    def _():
        early[...] = jnp.zeros_like(early)

    spectra(0)
    turn(0, 0)
    turn(0, 1)

    def core_copy(c):
        return pltpu.make_async_remote_copy(
            src_ref=p.at[c, 1 - core],
            dst_ref=r1.at[c],
            send_sem=c_send.at[c],
            recv_sem=c_recv.at[c],
            device_id={"grp": core_peer},
            device_id_type=MESH,
        )

    def y_copy(c, d):
        return pltpu.make_async_remote_copy(
            src_ref=p.at[c, core, (y + d) % 4],
            dst_ref=r2.at[c, d - 1],
            send_sem=y_send.at[c, d - 1],
            recv_sem=y_recv.at[c, d - 1],
            device_id={"grp": y_peer(d)},
            device_id_type=MESH,
        )

    def z_copy(c):
        return pltpu.make_async_remote_copy(
            src_ref=s3.at[c],
            dst_ref=r3.at[c],
            send_sem=z_send.at[c],
            recv_sem=z_recv.at[c],
            device_id={"grp": z_peer},
            device_id_type=MESH,
        )

    lanes = lax.broadcasted_iota(jnp.int32, (TILE, LANES), 1)
    quarter = LANES // 4
    scale = 1.0 / math.sqrt(frames * groups)
    order = [zz * 8 + yy * 2 + cc for cc in range(2) for yy in range(4) for zz in range(2)]
    tiles = v.shape[2] // TILE

    def zone(number):
        return jnp.where(lanes // quarter == number, scale, 0.0)

    def products(pair, which):
        c = pair * 2 + which
        keep_re, keep_im = zone(2 * which), zone(2 * which + 1)
        for r in range(tiles):
            left = []
            for h in range(2):
                value = v[h, pair, r * TILE : (r + 1) * TILE].astype(F32)
                plain = (value * (keep_re + keep_im)).reshape(16, 8, LANES)
                cross = pltpu.roll(value, LANES - quarter, 1) * keep_re - pltpu.roll(value, quarter, 1) * keep_im
                cross = cross.reshape(16, 8, LANES)
                left.append(jnp.concatenate([part for o in order for part in (plain[o], cross[o])], axis=0).astype(BF16))
            left = jnp.concatenate(left, axis=1)
            right = jnp.concatenate([v[h, pair, 0 : (r + 1) * TILE] for h in range(2)], axis=1)
            got = nt_dot(left, right).astype(BF16)
            for q in range(r + 1):
                t = r * (r + 1) // 2 + q
                p[c, :, :, :, t * 16 : (t + 1) * 16, :] = got[:, q * TILE : (q + 1) * TILE].reshape(2, 4, 2, 16, LANES)
        core_copy(c).start()

    def core_sum(c):
        core_copy(c).wait_recv()
        for yy in range(4):
            p[c, core, yy] = (p[c, core, yy].astype(F32) + r1[c, yy].astype(F32)).astype(BF16)
        for d in range(1, 4):
            y_copy(c, d).start()

    def y_sum(c):
        for d in range(1, 4):
            y_copy(c, d).wait_recv()
        for zz, mine in ((1 - z, False), (z, True)):
            got = p[c, core, y, zz].astype(F32)
            for d in range(3):
                got = got + r2[c, d, zz].astype(F32)
            if mine:
                keep[c] = got
            else:
                s3[c] = got.astype(BF16)
                z_copy(c).start()

    def gather(pair):
        for h in (1, 0):
            turn_wait(h, pair, a_recv)

    gather(0)
    products(0, 0)
    products(0, 1)
    core_sum(0)
    core_sum(1)
    y_sum(0)
    gather(1)
    products(1, 0)
    products(1, 1)
    core_sum(2)
    y_sum(1)
    core_sum(3)
    y_sum(2)
    y_sum(3)
    for c in range(channels):
        z_copy(c).wait_recv()
        got = keep[c] + r3[c].astype(F32)
        done[c] = got.reshape(done.shape[1:])
        for t in range(done.shape[1]):
            r, q = order_ref[0, t], order_ref[1, t]
            out_ref[c, t] = done[c, r * (r + 1) // 2 + q].reshape(out_ref.shape[2:])

    @pl.when(g < groups - 1)
    def _():
        tail_copy.wait_send()

    for h in range(2):
        for pair in range(2):
            turn_wait(h, pair, a_send)
    for c in range(channels):
        core_copy(c).wait_send()
        for d in range(1, 4):
            y_copy(c, d).wait_send()
        z_copy(c).wait_send()


def shards(samples, channel_index, tile_order):
    streams, length = samples.shape
    frames = length // FFT
    selected = channel_index.shape[0]
    channels = selected // lax.axis_size("inp")
    tile_count = tile_order.shape[0]
    rows = tile_count * 16
    vmem = pl.BlockSpec(memory_space=pltpu.VMEM)
    hbm = pl.BlockSpec(memory_space=pltpu.HBM)
    dma = pltpu.SemaphoreType.DMA
    all_streams = streams * lax.axis_size("inp")
    return pl.pallas_call(
        correlator_kernel,
        out_shape=jax.ShapeDtypeStruct((channels, tile_count, 2, 8, LANES), F32),
        in_specs=[vmem, pl.BlockSpec(memory_space=pltpu.SMEM), hbm, hbm],
        out_specs=vmem,
        scratch_shapes=[
            pltpu.VMEM((streams, length), BF16),
            pltpu.VMEM((TAPS, FFT), F32),
            pltpu.VMEM((selected, selected), jnp.int32),
            pltpu.VMEM((2 * selected, FFT), BF16),
            pltpu.VMEM((streams * frames // 2, FFT), BF16),
            pltpu.VMEM((2, streams * frames // 2, LANES), F32),
            pltpu.VMEM((selected // 2 * streams, LANES), F32),
            pltpu.VMEM((2, selected // 2 * streams, LANES), BF16),
            pltpu.VMEM((TAPS * streams, 2 * selected), BF16),
            pltpu.VMEM((TAPS * streams, 2 * selected), BF16),
            pltpu.VMEM((2, 2, all_streams, LANES), BF16),
            pltpu.VMEM((channels, 2, 4, 2, rows, LANES), BF16),
            pltpu.VMEM((channels, 4, 2, rows, LANES), BF16),
            pltpu.VMEM((channels, 3, 2, rows, LANES), BF16),
            pltpu.VMEM((channels, rows, LANES), F32),
            pltpu.VMEM((channels, rows, LANES), BF16),
            pltpu.VMEM((channels, rows, LANES), BF16),
            pltpu.VMEM((channels, tile_count, 16, LANES), F32),
            dma((4,)),
            dma((2,)),
            dma((2, 2)),
            dma((2, 2)),
            dma((channels,)),
            dma((channels,)),
            dma((channels, 3)),
            dma((channels, 3)),
            dma((channels,)),
            dma((channels,)),
        ],
        compiler_params=pltpu.CompilerParams(collective_id=0, has_side_effects=True, vmem_limit_bytes=61 * 1024 * 1024),
        name="correlator",
    )(channel_index.reshape(1, selected), tile_order.T, samples, jnp.asarray(pfb_window()))


def solution(mesh):
    in_specs = (P("inp", "grp"), P(), P())
    out_specs = P("inp", None, None, "grp", None)
    return jax.shard_map(shards, mesh=mesh, in_specs=in_specs, out_specs=out_specs, check_vma=False)
```

time: 91.8 us -> 78.3 us (0.85)
  the two profiles are of different devices: /device:TPU:52 before, /device:TPU:7 now
where the time goes in v2:
time: 78.3 us; the launch traced here: 78.1 us
  Pallas kernels  76.4 us (98%)
  local copies, waits for them, and re-layouts  1.72 us (2%)
    pallas_call x1, Pallas kernels, shards(): pl.pallas_call(correlator_kernel, out_shape=jax.ShapeDtypeStruct((channel...  76.4 us
    unnamed x1, local copies, waits for them, and re-layouts  1.72 us

profile of v2, /device:TPU:7, one launch (start us, length us, event | category | flops | bytes accessed | tf_op | source)
XLA Modules:
  0.0 78.1 jit_solution(5022819853541317150)
XLA Ops:
  0.0 76.4 %correlator.1 = f32[4,10,2,8,128]{4,3,2,1,0:T(8,128)} custom-call(s32[1,128]{1,0:T(1,128)} %bitcast.3, s32[2,10]{1,0:T(2,128)} %bitcast.2, bf16[16,131072]{1,0:T(8,128)(2,1)} %x_hbm.1, f32[16,2048]{1,0:T(8,128)} %constant.2.clone.w_hbm), custom_call_target="tpu_custom_call" | custom-call | tf_op jit(solution)/shard_map/correlator/pallas_call | solution.py:344
  76.4 1.7 %copy.6 = f32[4,10,2,8,128]{4,3,2,1,0:T(8,128)} copy(f32[4,10,2,8,128]{4,3,2,1,0:T(8,128)} %correlator.1) | data formatting | bytes 655360

commit v3 on v2

--- a/solution.py
+++ b/solution.py
@@ -66,7 +66,7 @@
     count = index_ref.shape[1]
     step = 2.0 * math.pi / FFT
     picked[...] = jnp.transpose(jnp.broadcast_to(index_ref[...], (count, count)))
-    channel = jnp.concatenate([picked[pl.ds(i, count // 2, stride=2), :] for i in range(2)], axis=0)
+    channel = jnp.concatenate([picked[pl.ds(i, count // 4, stride=4), :] for i in (0, 2, 1, 3)], axis=0)
     column = lax.broadcasted_iota(jnp.int32, (count, count), 1)
     fine = ((channel * column) & (FFT - 1)).astype(F32) * step
     coarse = ((channel * (column * LANES)) & (FFT - 1)).astype(F32) * step
@@ -82,11 +82,11 @@
 
 def correlator_kernel(
     index_ref, order_ref, x_hbm, w_hbm, out_ref,
-    x, w, picked, table, filt, dft, stage, send, tail, early, v, p, r1, r2, keep, s3, r3, done,
+    x, w, picked, table, filt, dft, stage, held, send, tail, early, v, p, r1, r2, keep, s3, r3, done,
     load, t_sem, a_send, a_recv, c_send, c_recv, y_send, y_recv, z_send, z_recv,
 ):
     peers, groups = lax.axis_size("inp"), lax.axis_size("grp")
-    channels = p.shape[0]
+    units, channels = p.shape[0], out_ref.shape[0]
     me, g = lax.axis_index("inp"), lax.axis_index("grp")
     core, y, z = g % 2, (g // 2) % 4, g // 8
     streams, frames = x.shape[0], x.shape[1] // FFT
@@ -145,7 +145,7 @@
         device_id_type=MESH,
     )
     parts[2].wait()
-    filtered(half, half, 0, CHUNKS // 2)
+    filtered(half, half, 0, CHUNKS // 8)
     pl.semaphore_wait(barrier, peers - 1 + 6)
 
     @pl.when(g < groups - 1)
@@ -153,6 +153,7 @@
         tail_copy.start()
 
     low = lax.broadcasted_iota(jnp.int32, (LANES // 2, LANES), 1) < LANES // 2
+    block = peers * streams
 
     def spectra(h):
         got = nt_dot(filt[...], table[...])
@@ -166,37 +167,51 @@
             even, odd = turned[: LANES // 2], turned[LANES // 2 :]
             stage[pl.ds(s, LANES // 2, stride=streams), :] = jnp.where(low, even, pltpu.roll(odd, LANES // 2, 1))
             stage[pl.ds(s + 1, LANES // 2, stride=streams), :] = jnp.where(low, pltpu.roll(even, LANES // 2, 1), odd)
-        send[h] = stage[...].astype(BF16)
-
-    def turn(h, pair):
+        send[1 - h] = stage[:block].astype(BF16)
+
+    def singles():
+        first, second = held[...], stage[block:]
+        narrow = lax.broadcasted_iota(jnp.int32, first.shape, 1) < LANES // 2
+        send[2] = jnp.where(narrow, first, pltpu.roll(second, LANES // 2, 1)).astype(BF16)
+        send[3] = jnp.where(narrow, pltpu.roll(first, LANES // 2, 1), second).astype(BF16)
+
+    def turn(b):
         def rows_of(j):
-            return pl.ds(pl.multiple_of((j * 2 + pair) * streams, streams), streams)
-
-        here = pl.ds(pl.multiple_of(me * streams, streams), streams)
-
-        def one(d, carry):
-            j = lax.rem(me + d, peers)
+            return pl.ds(pl.multiple_of(j * streams, streams), streams)
+
+        def start(j):
             pltpu.make_async_remote_copy(
-                src_ref=send.at[h, rows_of(j)],
-                dst_ref=v.at[h, pair, here],
-                send_sem=a_send.at[h, pair],
-                recv_sem=a_recv.at[h, pair],
+                src_ref=send.at[b, rows_of(j)],
+                dst_ref=v.at[b, rows_of(me)],
+                send_sem=a_send.at[b],
+                recv_sem=a_recv.at[b],
                 device_id={"inp": j},
                 device_id_type=MESH,
             ).start()
+
+        side, deep, wide = me // 16, me // 4 % 4, me % 4
+
+        def across_middle(t, carry):
+            start((1 - side) * 16 + (deep + t // 4) % 4 * 4 + (wide + t) % 4)
             return carry
 
-        lax.fori_loop(1, peers, one, 0)
-        v[h, pair, here] = send[h, rows_of(me)]
-
-    def turn_wait(h, pair, sem):
-        part = v.at[h, pair, pl.ds(0, (peers - 1) * streams)]
-        pltpu.make_async_copy(part, part, sem.at[h, pair]).wait()
-
-    filtered(half, half, CHUNKS // 2, CHUNKS)
+        def same_side(t, carry):
+            u = 15 - t
+            start(side * 16 + (deep + u // 4) % 4 * 4 + (wide + u) % 4)
+            return carry
+
+        lax.fori_loop(0, 16, across_middle, 0)
+        lax.fori_loop(0, 15, same_side, 0)
+        v[b, rows_of(me)] = send[b, rows_of(me)]
+
+    def turn_wait(b, sem):
+        part = v.at[b, pl.ds(0, (peers - 1) * streams)]
+        pltpu.make_async_copy(part, part, sem.at[b]).wait()
+
+    filtered(half, half, CHUNKS // 8, CHUNKS)
     spectra(1)
-    turn(1, 0)
-    turn(1, 1)
+    turn(0)
+    held[...] = stage[block:]
     parts[3].wait()
     filtered(0, half)
 
@@ -209,35 +224,35 @@
         early[...] = jnp.zeros_like(early)
 
     spectra(0)
-    turn(0, 0)
-    turn(0, 1)
-
-    def core_copy(c):
+    turn(1)
+    singles()
+
+    def core_copy(u):
         return pltpu.make_async_remote_copy(
-            src_ref=p.at[c, 1 - core],
-            dst_ref=r1.at[c],
-            send_sem=c_send.at[c],
-            recv_sem=c_recv.at[c],
+            src_ref=p.at[u, 1 - core],
+            dst_ref=r1.at[u],
+            send_sem=c_send.at[u],
+            recv_sem=c_recv.at[u],
             device_id={"grp": core_peer},
             device_id_type=MESH,
         )
 
-    def y_copy(c, d):
+    def y_copy(u, d):
         return pltpu.make_async_remote_copy(
-            src_ref=p.at[c, core, (y + d) % 4],
-            dst_ref=r2.at[c, d - 1],
-            send_sem=y_send.at[c, d - 1],
-            recv_sem=y_recv.at[c, d - 1],
+            src_ref=p.at[u, core, (y + d) % 4],
+            dst_ref=r2.at[u, d - 1],
+            send_sem=y_send.at[u, d - 1],
+            recv_sem=y_recv.at[u, d - 1],
             device_id={"grp": y_peer(d)},
             device_id_type=MESH,
         )
 
-    def z_copy(c):
+    def z_copy(u):
         return pltpu.make_async_remote_copy(
-            src_ref=s3.at[c],
-            dst_ref=r3.at[c],
-            send_sem=z_send.at[c],
-            recv_sem=z_recv.at[c],
+            src_ref=s3.at[u],
+            dst_ref=r3.at[u],
+            send_sem=z_send.at[u],
+            recv_sem=z_recv.at[u],
             device_id={"grp": z_peer},
             device_id_type=MESH,
         )
@@ -246,72 +261,87 @@
     quarter = LANES // 4
     scale = 1.0 / math.sqrt(frames * groups)
     order = [zz * 8 + yy * 2 + cc for cc in range(2) for yy in range(4) for zz in range(2)]
-    tiles = v.shape[2] // TILE
-
-    def zone(number):
-        return jnp.where(lanes // quarter == number, scale, 0.0)
-
-    def products(pair, which):
-        c = pair * 2 + which
-        keep_re, keep_im = zone(2 * which), zone(2 * which + 1)
+    tiles = v.shape[1] // TILE
+    part = out_ref.shape[1] // 2
+
+    def zone(*numbers):
+        return sum(jnp.where(lanes // quarter == number, scale, 0.0) for number in numbers)
+
+    def products(c):
+        batches = (0, 1) if c < 2 else (c,)
+        re, im = (zone(2 * c), zone(2 * c + 1)) if c < 2 else (zone(0, 2), zone(1, 3))
         for r in range(tiles):
             left = []
-            for h in range(2):
-                value = v[h, pair, r * TILE : (r + 1) * TILE].astype(F32)
-                plain = (value * (keep_re + keep_im)).reshape(16, 8, LANES)
-                cross = pltpu.roll(value, LANES - quarter, 1) * keep_re - pltpu.roll(value, quarter, 1) * keep_im
+            for b in batches:
+                value = v[b, r * TILE : (r + 1) * TILE].astype(F32)
+                plain = (value * (re + im)).reshape(16, 8, LANES)
+                cross = pltpu.roll(value, LANES - quarter, 1) * re - pltpu.roll(value, quarter, 1) * im
                 cross = cross.reshape(16, 8, LANES)
-                left.append(jnp.concatenate([part for o in order for part in (plain[o], cross[o])], axis=0).astype(BF16))
+                left.append(jnp.concatenate([piece for o in order for piece in (plain[o], cross[o])], axis=0).astype(BF16))
             left = jnp.concatenate(left, axis=1)
-            right = jnp.concatenate([v[h, pair, 0 : (r + 1) * TILE] for h in range(2)], axis=1)
+            right = jnp.concatenate([v[b, 0 : (r + 1) * TILE] for b in batches], axis=1)
             got = nt_dot(left, right).astype(BF16)
             for q in range(r + 1):
                 t = r * (r + 1) // 2 + q
-                p[c, :, :, :, t * 16 : (t + 1) * 16, :] = got[:, q * TILE : (q + 1) * TILE].reshape(2, 4, 2, 16, LANES)
-        core_copy(c).start()
-
-    def core_sum(c):
-        core_copy(c).wait_recv()
+                unit, at = c * 2 + t // part, t % part * 16
+                p[unit, :, :, :, at : at + 16, :] = got[:, q * TILE : (q + 1) * TILE].reshape(2, 4, 2, 16, LANES)
+            if r == tiles - 2:
+                core_copy(c * 2).start()
+        core_copy(c * 2 + 1).start()
+
+    def core_sum(u):
+        core_copy(u).wait_recv()
         for yy in range(4):
-            p[c, core, yy] = (p[c, core, yy].astype(F32) + r1[c, yy].astype(F32)).astype(BF16)
+            p[u, core, yy] = (p[u, core, yy].astype(F32) + r1[u, yy].astype(F32)).astype(BF16)
+        for d in (2, 1, 3):
+            y_copy(u, d).start()
+
+    def y_sum(u):
         for d in range(1, 4):
-            y_copy(c, d).start()
-
-    def y_sum(c):
-        for d in range(1, 4):
-            y_copy(c, d).wait_recv()
+            y_copy(u, d).wait_recv()
         for zz, mine in ((1 - z, False), (z, True)):
-            got = p[c, core, y, zz].astype(F32)
+            got = p[u, core, y, zz].astype(F32)
             for d in range(3):
-                got = got + r2[c, d, zz].astype(F32)
+                got = got + r2[u, d, zz].astype(F32)
             if mine:
-                keep[c] = got
+                keep[u] = got
             else:
-                s3[c] = got.astype(BF16)
-                z_copy(c).start()
-
-    def gather(pair):
-        for h in (1, 0):
-            turn_wait(h, pair, a_recv)
-
-    gather(0)
-    products(0, 0)
-    products(0, 1)
-    core_sum(0)
-    core_sum(1)
+                s3[u] = got.astype(BF16)
+                z_copy(u).start()
+
+    def z_sum(u):
+        z_copy(u).wait_recv()
+        done[u // 2, u % 2 * part : (u % 2 + 1) * part] = (keep[u] + r3[u].astype(F32)).reshape((part,) + done.shape[2:])
+
+    turn_wait(1, a_send)
+    turn(2)
+    turn_wait(0, a_recv)
+    turn_wait(1, a_recv)
+    products(0)
+    products(1)
+    turn_wait(2, a_send)
+    turn(3)
+    for u in (0, 1, 2, 3):
+        core_sum(u)
+    turn_wait(2, a_recv)
+    products(2)
     y_sum(0)
-    gather(1)
-    products(1, 0)
-    products(1, 1)
-    core_sum(2)
     y_sum(1)
-    core_sum(3)
+    core_sum(4)
+    core_sum(5)
+    turn_wait(3, a_recv)
+    products(3)
     y_sum(2)
     y_sum(3)
+    core_sum(6)
+    core_sum(7)
+    z_sum(0)
+    z_sum(1)
+    for u in (4, 5, 6, 7):
+        y_sum(u)
+    for u in (2, 3, 4, 5, 6, 7):
+        z_sum(u)
     for c in range(channels):
-        z_copy(c).wait_recv()
-        got = keep[c] + r3[c].astype(F32)
-        done[c] = got.reshape(done.shape[1:])
         for t in range(done.shape[1]):
             r, q = order_ref[0, t], order_ref[1, t]
             out_ref[c, t] = done[c, r * (r + 1) // 2 + q].reshape(out_ref.shape[2:])
@@ -320,14 +350,13 @@
     def _():
         tail_copy.wait_send()
 
-    for h in range(2):
-        for pair in range(2):
-            turn_wait(h, pair, a_send)
-    for c in range(channels):
-        core_copy(c).wait_send()
+    turn_wait(0, a_send)
+    turn_wait(3, a_send)
+    for u in range(units):
+        core_copy(u).wait_send()
         for d in range(1, 4):
-            y_copy(c, d).wait_send()
-        z_copy(c).wait_send()
+            y_copy(u, d).wait_send()
+        z_copy(u).wait_send()
 
 
 def shards(samples, channel_index, tile_order):
@@ -336,7 +365,8 @@
     selected = channel_index.shape[0]
     channels = selected // lax.axis_size("inp")
     tile_count = tile_order.shape[0]
-    rows = tile_count * 16
+    rows = tile_count // 2 * 16
+    units = 2 * channels
     vmem = pl.BlockSpec(memory_space=pltpu.VMEM)
     hbm = pl.BlockSpec(memory_space=pltpu.HBM)
     dma = pltpu.SemaphoreType.DMA
@@ -354,27 +384,28 @@
             pltpu.VMEM((streams * frames // 2, FFT), BF16),
             pltpu.VMEM((2, streams * frames // 2, LANES), F32),
             pltpu.VMEM((selected // 2 * streams, LANES), F32),
-            pltpu.VMEM((2, selected // 2 * streams, LANES), BF16),
+            pltpu.VMEM((all_streams, LANES), F32),
+            pltpu.VMEM((4, all_streams, LANES), BF16),
             pltpu.VMEM((TAPS * streams, 2 * selected), BF16),
             pltpu.VMEM((TAPS * streams, 2 * selected), BF16),
-            pltpu.VMEM((2, 2, all_streams, LANES), BF16),
-            pltpu.VMEM((channels, 2, 4, 2, rows, LANES), BF16),
-            pltpu.VMEM((channels, 4, 2, rows, LANES), BF16),
-            pltpu.VMEM((channels, 3, 2, rows, LANES), BF16),
-            pltpu.VMEM((channels, rows, LANES), F32),
-            pltpu.VMEM((channels, rows, LANES), BF16),
-            pltpu.VMEM((channels, rows, LANES), BF16),
+            pltpu.VMEM((4, all_streams, LANES), BF16),
+            pltpu.VMEM((units, 2, 4, 2, rows, LANES), BF16),
+            pltpu.VMEM((units, 4, 2, rows, LANES), BF16),
+            pltpu.VMEM((units, 3, 2, rows, LANES), BF16),
+            pltpu.VMEM((units, rows, LANES), F32),
+            pltpu.VMEM((units, rows, LANES), BF16),
+            pltpu.VMEM((units, rows, LANES), BF16),
             pltpu.VMEM((channels, tile_count, 16, LANES), F32),
             dma((4,)),
             dma((2,)),
-            dma((2, 2)),
-            dma((2, 2)),
-            dma((channels,)),
-            dma((channels,)),
-            dma((channels, 3)),
-            dma((channels, 3)),
-            dma((channels,)),
-            dma((channels,)),
+            dma((4,)),
+            dma((4,)),
+            dma((units,)),
+            dma((units,)),
+            dma((units, 3)),
+            dma((units, 3)),
+            dma((units,)),
+            dma((units,)),
         ],
         compiler_params=pltpu.CompilerParams(collective_id=0, has_side_effects=True, vmem_limit_bytes=61 * 1024 * 1024),
         name="correlator",

time: 78.3 us -> 73.1 us (0.934)
  the two profiles are of different devices: /device:TPU:7 before, /device:TPU:1 now
where the time goes in v3:
time: 73.1 us; the launch traced here: 72.9 us
  Pallas kernels  71.2 us (97%)
  local copies, waits for them, and re-layouts  1.72 us (2%)
    pallas_call x1, Pallas kernels, shards(): pl.pallas_call(correlator_kernel, out_shape=jax.ShapeDtypeStruct((channel...  71.2 us
    unnamed x1, local copies, waits for them, and re-layouts  1.72 us

profile of v3, /device:TPU:1, one launch (start us, length us, event | category | flops | bytes accessed | tf_op | source)
XLA Modules:
  0.0 72.9 jit_solution(275310158266355523)
XLA Ops:
  0.0 71.2 %correlator.1 = f32[4,10,2,8,128]{4,3,2,1,0:T(8,128)} custom-call(s32[1,128]{1,0:T(1,128)} %bitcast.3, s32[2,10]{1,0:T(2,128)} %bitcast.2, bf16[16,131072]{1,0:T(8,128)(2,1)} %x_hbm.1, f32[16,2048]{1,0:T(8,128)} %constant.2.clone.w_hbm), custom_call_target="tpu_custom_call" | custom-call | tf_op jit(solution)/shard_map/correlator/pallas_call | solution.py:374
  71.2 1.7 %copy.6 = f32[4,10,2,8,128]{4,3,2,1,0:T(8,128)} copy(f32[4,10,2,8,128]{4,3,2,1,0:T(8,128)} %correlator.1) | data formatting | bytes 655360

commit v4 on v3

--- a/solution.py
+++ b/solution.py
@@ -32,7 +32,7 @@
 
 
 def is_inner(tap):
-    return TAPS // 2 - 2 <= tap < TAPS // 2 + 2
+    return TAPS // 2 - 1 <= tap < TAPS // 2 + 1
 
 
 def fir(x_ref, w_ref, filt, at, first, count, row):
@@ -313,34 +313,52 @@
         z_copy(u).wait_recv()
         done[u // 2, u % 2 * part : (u % 2 + 1) * part] = (keep[u] + r3[u].astype(F32)).reshape((part,) + done.shape[2:])
 
+    def y_left(u):
+        for d in range(1, 4):
+            y_copy(u, d).wait_send()
+
     turn_wait(1, a_send)
     turn(2)
     turn_wait(0, a_recv)
     turn_wait(1, a_recv)
     products(0)
     products(1)
+    core_sum(0)
+    core_sum(1)
     turn_wait(2, a_send)
     turn(3)
-    for u in (0, 1, 2, 3):
-        core_sum(u)
     turn_wait(2, a_recv)
     products(2)
+    y_left(0)
+    y_left(1)
+    core_sum(2)
+    core_sum(3)
     y_sum(0)
     y_sum(1)
+    y_left(2)
+    y_left(3)
     core_sum(4)
     core_sum(5)
     turn_wait(3, a_recv)
     products(3)
     y_sum(2)
     y_sum(3)
+    y_left(4)
+    y_left(5)
     core_sum(6)
     core_sum(7)
+    y_sum(4)
+    y_sum(5)
+    y_sum(6)
+    y_sum(7)
     z_sum(0)
     z_sum(1)
-    for u in (4, 5, 6, 7):
-        y_sum(u)
-    for u in (2, 3, 4, 5, 6, 7):
-        z_sum(u)
+    z_sum(2)
+    z_sum(3)
+    z_sum(4)
+    z_sum(5)
+    z_sum(6)
+    z_sum(7)
     for c in range(channels):
         for t in range(done.shape[1]):
             r, q = order_ref[0, t], order_ref[1, t]
@@ -354,8 +372,8 @@
     turn_wait(3, a_send)
     for u in range(units):
         core_copy(u).wait_send()
-        for d in range(1, 4):
-            y_copy(u, d).wait_send()
+        if u >= 6:
+            y_left(u)
         z_copy(u).wait_send()
 
 

time: 73.1 us -> 71.8 us (0.982)
  Pallas kernels: 71.2 us -> 69.9 us
    pallas_call x1, Pallas kernels: 71.2 us -> 69.9 us  [shards(): pl.pallas_call(correlator_kernel, out_shape=jax.ShapeDtypeStruct((channel...]
where the time goes in v4:
time: 71.8 us; the launch traced here: 71.6 us
  Pallas kernels  69.9 us (97%)
  local copies, waits for them, and re-layouts  1.72 us (2%)
    pallas_call x1, Pallas kernels, shards(): pl.pallas_call(correlator_kernel, out_shape=jax.ShapeDtypeStruct((channel...  69.9 us
    unnamed x1, local copies, waits for them, and re-layouts  1.72 us

profile of v4, /device:TPU:1, one launch (start us, length us, event | category | flops | bytes accessed | tf_op | source)
XLA Modules:
  0.0 71.6 jit_solution(17191785194524782227)
XLA Ops:
  0.0 69.9 %correlator.1 = f32[4,10,2,8,128]{4,3,2,1,0:T(8,128)} custom-call(s32[1,128]{1,0:T(1,128)} %bitcast.3, s32[2,10]{1,0:T(2,128)} %bitcast.2, bf16[16,131072]{1,0:T(8,128)(2,1)} %x_hbm.1, f32[16,2048]{1,0:T(8,128)} %constant.2.clone.w_hbm), custom_call_target="tpu_custom_call" | custom-call | tf_op jit(solution)/shard_map/correlator/pallas_call | solution.py:392
  69.9 1.7 %copy.6 = f32[4,10,2,8,128]{4,3,2,1,0:T(8,128)} copy(f32[4,10,2,8,128]{4,3,2,1,0:T(8,128)} %correlator.1) | data formatting | bytes 655360
